TPU v7x, 32 devices: a whole 2x2x4 slice. The times are simulated.
32 devices in a mesh: row: 4 (over z), col: 8 (over y, x, core).
Axes of the slice: x: 2, y: 2, z: 4, core: 2. Of those that a mesh axis runs over, the one named last changes fastest.
Arguments:
- ancestor: float32 [24576, 24576], P('row', 'col'), may hold values from -6 to 6
- lhat_one: float32 [24576, 512], P('col', 'row'), may hold values from -0.109375 to 0.109375
- lhat_two: float32 [24576, 512], P('col', 'row'), may hold values from -0.109375 to 0.109375
- link_two: float32 [512, 512], replicated, may hold values from -0.25 to 0.25
- diag_one: float32 [512, 512], replicated, may hold values from -6 to 6
- diag_two: float32 [512, 512], replicated, may hold values from -6 to 6
- mask_one: int32 [192], replicated, may hold values from 0 to 1, as said below
- mask_two: int32 [192], replicated, may hold values from 0 to 1, as said below
Outputs:
- x_one: float32 [24576, 512], P('row', 'col')
- d_one: float32 [512, 512], replicated
- x_two: float32 [24576, 512], P('row', 'col')
- link_inverse: float32 [512, 512], replicated
- d_two: float32 [512, 512], replicated
Inputs may be any that keep to these rules, and one draw needn't show every extreme that they name: `mask_one`: 1 where a block of 128 factor rows is nonzero, else 0; the last block is always nonzero. `mask_two`: 1 where a block of 128 factor rows is nonzero, else 0; the last block is always nonzero.
All inputs are finite; a program needn't handle non-finite values.
Results may differ from a plain program's by a relative error of at most 0.00011.
Values sent between devices are 32-bit elements; how exact they have to be, the bound alone decides.
A program may use at most 192 MiB of HBM per device.

v0:
```python
import jax
import jax.numpy as jnp
from jax import lax
from jax.sharding import PartitionSpec as P

BLOCK = 128


def product(left, right):
    return jnp.dot(left, right, precision=lax.Precision.HIGHEST, preferred_element_type=jnp.float32)


def per_device(ancestor, lhat_one, lhat_two, link_two, diag_one, diag_two, mask_one, mask_two):
    column_index = lax.axis_index("col")
    row_index = lax.axis_index("row")
    row_count = lax.axis_size("row")
    column_count = lax.axis_size("col")
    column_rows = lhat_one.shape[0]
    sub_rows = column_rows // row_count
    share_rows = sub_rows // row_count
    full_width = link_two.shape[0]
    column_width = full_width // column_count
    blocks = column_rows // BLOCK

    def factor(factor_part, block_mask):
        complete = lax.all_gather(factor_part, "row", axis=1, tiled=True)
        mask_part = lax.dynamic_slice_in_dim(block_mask, column_index * blocks, blocks)
        expanded = jnp.repeat(mask_part.astype(jnp.float32), BLOCK, total_repeat_length=column_rows)
        return complete * expanded[:, None]

    def row_sum(partial_value):
        own_part = -lax.psum_scatter(partial_value, "col", scatter_dimension=1, tiled=True)
        complete = lax.all_gather(own_part, "col", axis=1, tiled=True)
        return (own_part, complete)

    def mirror(complete):
        parity = column_index % 2
        section = lax.dynamic_slice_in_dim(complete, parity * column_rows, column_rows, 0)
        section = section.reshape(row_count, sub_rows, full_width)
        outgoing = lax.dynamic_slice_in_dim(section, column_index // 2 * share_rows, share_rows, 1)
        arrived = lax.all_to_all(outgoing, "row", split_axis=0, concat_axis=0, tiled=True)
        parity_mask = (jnp.arange(2, dtype=jnp.int32) == parity).astype(jnp.float32)
        spread = arrived[:, None, :, :] * parity_mask[None, :, None, None]
        spread = spread.reshape(column_count, share_rows, full_width)
        landed = lax.all_to_all(spread, "col", split_axis=0, concat_axis=0, tiled=True)
        landed = landed.reshape(row_count, 2, share_rows, full_width)
        chosen = lax.dynamic_index_in_dim(landed, parity, 1, keepdims=False)
        return chosen.reshape(sub_rows, full_width)

    def rows_of(matrix):
        return lax.dynamic_slice_in_dim(matrix, row_index * sub_rows, sub_rows, 0)

    factor_one = factor(lhat_one, mask_one)
    x_one, complete_one = row_sum(product(ancestor, factor_one))
    factor_two = factor(lhat_two, mask_two)
    link_rows = lax.dynamic_slice_in_dim(link_two, column_index * column_width, column_width, 0)
    mirrored_one = mirror(complete_one)
    ancestor_two = product(ancestor, factor_two)
    ancestor_two = ancestor_two + product(x_one, link_rows)
    factor_sub_one = rows_of(factor_one)
    factor_sub_two = rows_of(factor_two)
    column_diag, column_link = lax.psum(
        (product(factor_sub_one.T, mirrored_one), product(mirrored_one.T, factor_sub_two)), "row"
    )
    diag_part, link_part = lax.psum((column_diag, column_link), "col")
    d_one = diag_one - diag_part
    link_inverse = -(link_part + product(d_one, link_two))
    x_two, complete_two = row_sum(ancestor_two)
    mirrored_two = mirror(complete_two)
    column_last = lax.psum(product(factor_sub_two.T, mirrored_two), "row")
    last_part = lax.psum(column_last, "col")
    d_two = diag_two - last_part - product(link_two.T, link_inverse)
    return (x_one, d_one, x_two, link_inverse, d_two)


def solution(mesh):
    in_specs = (P("row", "col"), P("col", "row"), P("col", "row"), P(), P(), P(), P(), P())
    out_specs = (P("row", "col"), P(), P("row", "col"), P(), P())
    return jax.shard_map(
        per_device, mesh=mesh, in_specs=in_specs, out_specs=out_specs, check_vma=False
    )
```

profile of v0, /device:TPU:0, one launch (start us, length us, event | category | flops | bytes accessed | tf_op | source)
XLA Modules:
  0.0 1268.2 jit_solution(11433145355435041794)
XLA Ops:
  10.8 15.2 %select_select_fusion.1 = f32[3072]{0:T(1024)S(1)} fusion(f32[]{:T(128)} %bitcast.24, f32[]{:T(128)} %bitcast.23, f32[]{:T(128)} %bitcast.22, f32[]{:T(128)} %bitcast.21, f32[]{:T(128)} %bitcast.20, f32[]{:T(128)} %bitcast.19, f32[]{:T(128)} %bitcast.18, f32[]{:T(128)} %bitcast.17, f32[]{:T(128)} %bitcast.16, f32[]{:T(128)} %bitcast.15, f32[]{:T(128)} %bitcast.14, ...), kind=kLoop, calls=%fused_computation.19 | loop fusion | flops 168960 | bytes 12384 | tf_op jit(solution)/shard_map/jit(_take)/select_n | solution.py:28
  26.0 101.1 %all-gather.5.cloned.1.call-done = f32[3072,512]{1,0:T(8,128)} async-done(((f32[3072,128]{1,0:T(8,128)}), f32[3072,512]{1,0:T(8,128)}) %all-gather.5.cloned.1.call-update) | async-done | bytes 6291472 | tf_op jit(solution)/shard_map/all_gather | solution.py:26
  127.2 5.9 broadcast_multiply_fusion.1
  133.0 242.5 %convolution_bitcast_fusion = f32[6144,512]{0,1:T(8,128)} fusion(f32[3072,512]{1,0:T(8,128)} %broadcast_multiply_fusion.1, f32[6144,3072]{1,0:T(8,128)} %param.14), kind=kOutput, calls=%fused_computation.1 | convolution fusion | flops 115964116992 | bytes 94371840 | tf_op jit(solution)/shard_map/dot_general | solution.py:10
  376.9 15.2 %select_select_fusion = f32[3072]{0:T(1024)S(1)} fusion(f32[]{:T(128)} %bitcast.53, f32[]{:T(128)} %bitcast.52, f32[]{:T(128)} %bitcast.51, f32[]{:T(128)} %bitcast.50, f32[]{:T(128)} %bitcast.49, f32[]{:T(128)} %bitcast.48, f32[]{:T(128)} %bitcast.47, f32[]{:T(128)} %bitcast.46, f32[]{:T(128)} %bitcast.45, f32[]{:T(128)} %bitcast.44, f32[]{:T(128)} %bitcast.43, ...), kind=kLoop, calls=%fused_computation.18 | loop fusion | flops 168960 | bytes 12384 | tf_op jit(solution)/shard_map/jit(_take)/select_n | solution.py:28
  392.2 6.2 broadcast_multiply_fusion
  398.4 254.8 %fusion.43 = f32[512,6144]{1,0:T(8,128)} fusion(f32[3072,512]{1,0:T(8,128)} %broadcast_multiply_fusion, f32[6144,3072]{1,0:T(8,128)} %param.14), kind=kOutput, calls=%fused_computation.63 | convolution fusion | flops 115964116992 | bytes 94371840 | tf_op jit(solution)/shard_map/dot_general | solution.py:10
  654.8 15.3 %bitcast_add_fusion = f32[6144,512]{0,1:T(8,128)} fusion(f32[512,6144]{1,0:T(8,128)} %fusion.43, f32[6144,64]{0,1:T(8,128)S(1)} %neg.9, f32[512,512]{1,0:T(8,128)S(1)} %copy-done, s32[]{:T(128)S(6)} %select_n.55), kind=kOutput, calls=%fused_computation | convolution fusion | flops 2419064832 | bytes 26869764 | tf_op jit(solution)/shard_map/dot_general | solution.py:10
  670.7 90.6 %reduce-scatter.5.cloned.1.call-done = f32[6144,64]{0,1:T(8,128)} async-done(((f32[6144,512]{0,1:T(8,128)}), f32[6144,64]{0,1:T(8,128)}) %reduce-scatter.5.cloned.1.call-update) | async-done | bytes 1572880 | tf_op jit(solution)/shard_map/reduce_scatter | solution.py:32
  761.3 2.7 neg.10
  764.0 71.7 %all-gather.7.cloned.1.call-done = f32[6144,512]{0,1:T(8,128)} async-done(((f32[6144,64]{0,1:T(8,128)}), f32[6144,512]{0,1:T(8,128)}) %all-gather.7.cloned.1.call-update) | async-done | bytes 12582928 | tf_op jit(solution)/shard_map/all_gather | solution.py:33
  835.8 6.2 constant_dynamic-slice_fusion.5
  842.0 6.9 copy.14
  848.9 2.7 constant_dynamic-slice_fusion.4
  851.6 4.6 all-to-all-start
  856.2 54.0 %all-gather.11.cloned.1.call-done = f32[6144,512]{0,1:T(8,128)} async-done(((f32[6144,64]{0,1:T(8,128)}), f32[6144,512]{0,1:T(8,128)}) %all-gather.11.cloned.1.call-update) | async-done | bytes 12582928 | tf_op jit(solution)/shard_map/all_gather | solution.py:33
  910.2 6.1 constant_dynamic-slice_fusion.2
  916.4 6.6 copy.15
  923.0 2.7 constant_dynamic-slice_fusion.1
  925.6 4.6 all-to-all-start.2
  930.3 37.4 %all-to-all-done.2 = f32[4,192,512]{2,1,0:T(8,128)} async-done(((f32[4,192,512]{2,1,0:T(8,128)}), f32[4,192,512]{2,1,0:T(8,128)}, u32[]{:S(2)}, u32[]{:S(2)}) %all-to-all-start.2) | async-done | bytes 1572896 | tf_op jit(solution)/shard_map/all_to_all | solution.py:41
  967.7 3.6 bitcast_multiply_fusion
  971.4 41.0 %all_to_all.20 = f32[8,192,512]{2,1,0:T(8,128)} all-to-all(f32[8,192,512]{2,1,0:T(8,128)S(1)} %get-tuple-element.33), channel_id=1, replica_groups=mesh['row'=4,'col'=8] {'col'}, dimensions={0} | all-to-all | bytes 6291456 | tf_op jit(solution)/shard_map/all_to_all | solution.py:45
  1012.4 4.5 all-to-all-start.3
  1018.5 5.2 fusion.4
  1023.6 5.1 fusion
  1028.7 26.1 %all-to-all-done.3 = f32[8,192,512]{2,1,0:T(8,128)} async-done(((f32[8,192,512]{2,1,0:T(8,128)}), f32[8,192,512]{2,1,0:T(8,128)}, u32[]{:S(2)}, u32[]{:S(2)}) %all-to-all-start.3) | async-done | bytes 3145760 | tf_op jit(solution)/shard_map/all_to_all | solution.py:45
  1056.4 5.1 fusion.2
  1061.7 119.0 %all-reduce.7.cloned.1.call-done = (f32[512,512]{1,0:T(8,128)}, f32[512,512]{1,0:T(8,128)}, f32[512,512]{1,0:T(8,128)}) async-done(((f32[512,512]{1,0:T(8,128)}, f32[512,512]{1,0:T(8,128)}, f32[512,512]{1,0:T(8,128)}), (f32[512,512]{1,0:T(8,128)}, f32[512,512]{1,0:T(8,128)}, f32[512,512]{1,0:T(8,128)})) %all-reduce.7.cloned.1.call-update) | async-done | bytes 3145744 | tf_op jit(solution)/shard_map/psum | solution.py:62
  1180.7 72.5 %all-reduce.5.cloned.1.call-done = (f32[512,512]{1,0:T(8,128)}, f32[512,512]{1,0:T(8,128)}, f32[512,512]{1,0:T(8,128)}) async-done(((f32[512,512]{1,0:T(8,128)}, f32[512,512]{1,0:T(8,128)}, f32[512,512]{1,0:T(8,128)}), (f32[512,512]{1,0:T(8,128)}, f32[512,512]{1,0:T(8,128)}, f32[512,512]{1,0:T(8,128)})) %all-reduce.5.cloned.1.call-update) | async-done | bytes 3145744 | tf_op jit(solution)/shard_map/psum | solution.py:65
  1254.7 3.5 fusion.7
  1258.3 2.9 fusion.6
  (45 shorter events, 12.3 us)
Async XLA Ops:
  7.2 647.6 %copy-start = (f32[512,512]{1,0:T(8,128)S(1)}, f32[512,512]{1,0:T(8,128)}, u32[]{:S(2)}) copy-start(f32[512,512]{1,0:T(8,128)} %param.17) | copy-start | bytes 3145732
  7.2 120.0 %all-gather.5.cloned.1.call-start = ((), (), s32[]{:S(2)}) async-start(), calls=%async_computation.6 | async-start | bytes 7864320 | tf_op jit(solution)/shard_map/all_gather | solution.py:26
  7.9 384.2 %all-gather.9.cloned.1.call-start = ((), (), s32[]{:S(2)}) async-start(), calls=%async_computation.9 | async-start | bytes 7864320 | tf_op jit(solution)/shard_map/all_gather | solution.py:26
  8.7 644.5 %reduce-scatter.3.cloned.1.call-start = ((), (), s32[]{:S(2)}) async-start(), calls=%async_computation.7 | async-start | bytes 14155776 | tf_op jit(solution)/shard_map/reduce_scatter | solution.py:32
  375.6 385.7 %reduce-scatter.5.cloned.1.call-start = ((), (), s32[]{:S(2)}) async-start(), calls=%async_computation.10 | async-start | bytes 14155776 | tf_op jit(solution)/shard_map/reduce_scatter | solution.py:32
  654.7 15.3 %copy-start.1 = (f32[6144,64]{0,1:T(8,128)}, f32[6144,64]{0,1:T(8,128)S(1)}, u32[]{:S(2)}) copy-start(f32[6144,64]{0,1:T(8,128)S(1)} %neg.9) | copy-start | bytes 4718596
  670.0 165.7 %all-gather.7.cloned.1.call-start = ((), (), s32[]{:S(2)}) async-start(), calls=%async_computation.8 | async-start | bytes 14155776 | tf_op jit(solution)/shard_map/all_gather | solution.py:33
  670.6 239.6 %all-gather.11.cloned.1.call-start = ((), (), s32[]{:S(2)}) async-start(), calls=%async_computation.11 | async-start | bytes 14155776 | tf_op jit(solution)/shard_map/all_gather | solution.py:33
  851.6 74.0 %all-to-all-start = ((f32[4,192,512]{2,1,0:T(8,128)}), f32[4,192,512]{2,1,0:T(8,128)S(1)}, u32[]{:S(2)}, u32[]{:S(2)}) async-start(f32[4,192,512]{2,1,0:T(8,128)} %constant_dynamic-slice_fusion.4), calls=%async_computation.1 | async-start | bytes 3145728 | tf_op jit(solution)/shard_map/all_to_all | solution.py:41
  925.6 42.1 %all-to-all-start.2 = ((f32[4,192,512]{2,1,0:T(8,128)}), f32[4,192,512]{2,1,0:T(8,128)}, u32[]{:S(2)}, u32[]{:S(2)}) async-start(f32[4,192,512]{2,1,0:T(8,128)} %constant_dynamic-slice_fusion.1), calls=%async_computation.4 | async-start | bytes 3145728 | tf_op jit(solution)/shard_map/all_to_all | solution.py:41
  1012.4 42.3 %all-to-all-start.3 = ((f32[8,192,512]{2,1,0:T(8,128)}), f32[8,192,512]{2,1,0:T(8,128)}, u32[]{:S(2)}, u32[]{:S(2)}) async-start(f32[8,192,512]{2,1,0:T(8,128)} %get-tuple-element.32), calls=%async_computation.5 | async-start | bytes 6291456 | tf_op jit(solution)/shard_map/all_to_all | solution.py:45
  1016.9 163.8 %all-reduce.7.cloned.1.call-start = ((), (), s32[]{:S(2)}) async-start(), calls=%async_computation.13 | async-start | bytes 6291456 | tf_op jit(solution)/shard_map/psum | solution.py:62
  1054.8 198.4 %copy-start.4 = (f32[512,512]{1,0:T(8,128)S(1)}, f32[512,512]{1,0:T(8,128)}, u32[]{:S(2)}) copy-start(f32[512,512]{1,0:T(8,128)} %param.18) | copy-start | bytes 3145732
  1061.5 196.8 %copy-start.5 = (f32[512,512]{1,0:T(8,128)S(1)}, f32[512,512]{1,0:T(8,128)}, u32[]{:S(2)}) copy-start(f32[512,512]{1,0:T(8,128)} %param.19) | copy-start | bytes 3145732
  1061.5 191.7 %all-reduce.5.cloned.1.call-start = ((), (), s32[]{:S(2)}) async-start(), calls=%async_computation.12 | async-start | bytes 6291456 | tf_op jit(solution)/shard_map/psum | solution.py:65
  1253.2 5.1 copy-start.6
  1254.7 6.5 copy-start.2
  1258.3 2.9 copy-start.3
Sparse Core Ops, SparseCore 0:
  9.6 117.5 all-gather.4
  128.7 113.0 all-gather.8
  375.7 90.5 reduce-scatter.2
  670.2 91.0 reduce-scatter.4
  763.6 72.0 all-gather.6
  838.1 72.1 all-gather.10
  1061.6 119.0 all-reduce.6
  1184.3 68.8 all-reduce.4
where the time goes:
time: 1280 us; the launch traced here: 1270 us
  waiting for transfers between devices  574 us (45%)
  matrix products  534 us (42%)
  other arithmetic  52.6 us (4%)
  blocking collectives  41 us (3%)
  local copies, waits for them, and re-layouts  37.2 us (3%)
  between operations  14.5 us (1%)
  starting transfers between devices  14.2 us (1%)
    dot_general x8, matrix products, product(): jnp.dot(left, right, precision=lax.Precision.HIGHEST, preferred_element_t...  534 us
    all_gather x2, waiting for transfers between devices, row_sum(): complete = lax.all_gather(own_part, 'col', axis=1, tiled=True)  126 us
    psum x1, waiting for transfers between devices, per_device(): lax.psum((product(factor_sub_one.T, mirrored_one), product(mirrored_one.T...  119 us
    all_gather x2, waiting for transfers between devices, factor(): complete = lax.all_gather(factor_part, 'row', axis=1, tiled=True)  101 us
    reduce_scatter x2, waiting for transfers between devices, row_sum(): lax.psum_scatter(partial_value, 'col', scatter_dimension=1, tiled=True)  90.6 us
    psum x1, waiting for transfers between devices, per_device(): diag_part, link_part = lax.psum((column_diag, column_link), 'col')  72.5 us
    all_to_all x1, blocking collectives, mirror(): lax.all_to_all(spread, 'col', split_axis=0, concat_axis=0, tiled=True)  41 us
    all_to_all x2, waiting for transfers between devices, mirror(): lax.all_to_all(outgoing, 'row', split_axis=0, concat_axis=0, tiled=True)  37.4 us
  transfers between devices with their start and end apart: 11, of which 8 were waited for; matrix products, arithmetic and copies ran while one was open for 46% of the time, Pallas kernels for 0%

commit v1 on v0

v1 whole, which is shorter than its diff:
```python
import functools

import jax
import jax.numpy as jnp
from jax import lax
from jax.experimental import pallas as pl
from jax.experimental.pallas import tpu as pltpu
from jax.sharding import PartitionSpec as P

BLOCK = 128
PIECES = 2
NT = (((1,), (1,)), ((), ()))


def product(left, right):
    return jnp.dot(left, right, precision=lax.Precision.HIGHEST, preferred_element_type=jnp.float32)


def product_nt(left, right):
    return lax.dot_general(
        left, right, NT, precision=lax.Precision.HIGHEST, preferred_element_type=jnp.float32
    )


def halves(value):
    high = value.astype(jnp.bfloat16)
    low = (value - high.astype(jnp.float32)).astype(jnp.bfloat16)
    return high, low


def ancestor_kernel(factor_ref, ancestor_ref, out_ref, high_ref, low_ref):
    @pl.when(pl.program_id(0) == 0)
    def _():
        high, low = halves(factor_ref[...])
        high_ref[...] = high
        low_ref[...] = low

    left_high, left_low = halves(ancestor_ref[...])
    dot = functools.partial(
        lax.dot_general, dimension_numbers=NT, preferred_element_type=jnp.float32
    )
    total = dot(left_high, low_ref[...]) + dot(left_low, high_ref[...])
    total = total + dot(left_high, high_ref[...])
    out_ref[...] = total.T


def ancestor_product(factor, ancestor):
    wide, depth = factor.shape
    rows = ancestor.shape[0]
    tile = min(512, rows)
    return pl.pallas_call(
        ancestor_kernel,
        grid=(rows // tile,),
        out_shape=jax.ShapeDtypeStruct((wide, rows), jnp.float32),
        in_specs=[
            pl.BlockSpec((wide, depth), lambda i: (0, 0)),
            pl.BlockSpec((tile, depth), lambda i: (i, 0)),
        ],
        out_specs=pl.BlockSpec((wide, tile), lambda i: (0, i)),
        scratch_shapes=[pltpu.VMEM((wide, depth), jnp.bfloat16)] * 2,
        compiler_params=pltpu.CompilerParams(vmem_limit_bytes=48 * 1024 * 1024),
        cost_estimate=pl.CostEstimate(
            flops=6 * wide * depth * rows,
            bytes_accessed=4 * (rows * depth + wide * depth + wide * rows),
            transcendentals=0,
        ),
    )(factor, ancestor)


def per_device(ancestor, lhat_one, lhat_two, link_two, diag_one, diag_two, mask_one, mask_two):
    column_index = lax.axis_index("col")
    row_count = lax.axis_size("row")
    column_count = lax.axis_size("col")
    column_rows = lhat_one.shape[0]
    ancestor_rows = ancestor.shape[0]
    full_width = link_two.shape[0]
    own_width = full_width // column_count
    piece = own_width // PIECES
    share = piece // row_count
    blocks = column_rows // BLOCK
    bits = column_count.bit_length() - 1

    def factor(factor_part, block_mask):
        mask_part = lax.dynamic_slice_in_dim(block_mask, column_index * blocks, blocks)
        expanded = jnp.repeat(-mask_part.astype(jnp.float32), BLOCK, total_repeat_length=column_rows)
        part = (factor_part * expanded[:, None]).T
        part = part.reshape(-1, PIECES, piece, column_rows)
        return [
            lax.all_gather(part[:, q], "row", axis=0, tiled=True).reshape(-1, column_rows)
            for q in range(PIECES)
        ]

    def exchange(value, order, remaining):
        for bit in order:
            axis = remaining.index(bit)
            remaining = remaining[:axis] + remaining[axis + 1:]
            mine = (column_index >> bit) & 1
            outgoing = lax.dynamic_index_in_dim(value, 1 - mine, axis, keepdims=False)
            kept = lax.dynamic_index_in_dim(value, mine, axis, keepdims=False)
            pairs = [(i, i ^ (1 << bit)) for i in range(column_count)]
            value = kept + lax.ppermute(outgoing, "col", pairs)
        return value, remaining

    def row_sum(partial_value):
        value = partial_value.reshape((2,) * bits + (piece, ancestor_rows))
        value, remaining = exchange(value, (0,), tuple(reversed(range(bits))))
        upper, lower = value[..., : piece // 2, :], value[..., piece // 2:, :]
        upward = tuple(range(1, bits))
        upper, _ = exchange(upper, upward, remaining)
        lower, _ = exchange(lower, upward[::-1], remaining)
        return jnp.concatenate([upper, lower], axis=0)

    def mirror(own):
        outgoing = own.reshape(row_count, share, ancestor_rows)
        arrived = lax.all_to_all(outgoing, "row", split_axis=0, concat_axis=0, tiled=True)
        spread = arrived.reshape(row_count, share, column_count // row_count, column_rows)
        spread = spread.transpose(0, 2, 1, 3).reshape(column_count, share, column_rows)
        landed = lax.all_to_all(spread, "col", split_axis=0, concat_axis=0, tiled=True)
        return landed.reshape(column_count * share, column_rows)

    def device_sum(partial_value):
        width = partial_value.shape[1]
        outgoing = partial_value.reshape(column_count, -1, width)
        arrived = lax.all_to_all(outgoing, "col", split_axis=0, concat_axis=0, tiled=True)
        mine = jnp.sum(arrived, axis=0)
        complete = lax.all_gather(mine, ("row", "col"), axis=0, tiled=True)
        complete = complete.reshape(row_count, PIECES, column_count, share, -1, PIECES, column_count, piece)
        complete = complete.transpose(4, 2, 1, 0, 3, 6, 5, 7)
        return complete.reshape(-1, full_width, full_width)

    link_ordered = link_two.reshape(column_count, PIECES, piece, full_width)
    link_ordered = link_ordered.transpose(1, 0, 2, 3).reshape(full_width, full_width)
    link_columns = link_ordered.T.reshape(column_count, PIECES, piece, full_width)

    pieces_one = factor(lhat_one, mask_one)
    pieces_two = factor(lhat_two, mask_two)
    own_one = [row_sum(ancestor_product(part, ancestor)) for part in pieces_one]
    minus_one = jnp.concatenate(pieces_one, axis=0)
    own_two = []
    for q in range(PIECES):
        columns = link_columns[:, q].reshape(-1, full_width)
        combined = pieces_two[q] - product(columns, minus_one)
        own_two.append(row_sum(ancestor_product(combined, ancestor)))
    minus_two = jnp.concatenate(pieces_two, axis=0)

    mirrored_one = jnp.concatenate([mirror(own) for own in own_one], axis=0)
    first = jnp.concatenate(
        [product_nt(mirrored_one, minus_one), product_nt(mirrored_one, minus_two)], axis=1
    )
    diag_part, link_part = device_sum(first)
    d_one = diag_one + diag_part.T
    link_inverse = link_part - product(d_one, link_two)
    base_two = diag_two - product(link_two.T, link_inverse)

    last = jnp.concatenate([product_nt(mirror(own), minus_two) for own in own_two], axis=0)
    d_two = base_two + device_sum(last)[0].T
    x_one = jnp.concatenate(own_one, axis=0).T
    x_two = jnp.concatenate(own_two, axis=0).T
    return (x_one, d_one, x_two, link_inverse, d_two)


def solution(mesh):
    in_specs = (P("row", "col"), P("col", "row"), P("col", "row"), P(), P(), P(), P(), P())
    out_specs = (P("row", "col"), P(), P("row", "col"), P(), P())
    return jax.shard_map(
        per_device, mesh=mesh, in_specs=in_specs, out_specs=out_specs, check_vma=False
    )
```

time: 1280 us -> 820 us (0.64)
  matrix products: 534 us -> 54.8 us
  waiting for transfers between devices: 574 us -> 333 us
  Pallas kernels: 0 us -> 154 us
  local copies, waits for them, and re-layouts: 37.2 us -> 102 us
  starting transfers between devices: 14.2 us -> 55.7 us
  other arithmetic: 52.6 us -> 68.8 us
    dot_general x8 -> x4, matrix products: 534 us -> 21.5 us  [product(): jnp.dot(left, right, precision=lax.Precision.HIGHEST, preferred_element_t...]
    psum x2 -> x0, waiting for transfers between devices: 191 us -> none  [the longest x1 119 us: per_device(): lax.psum((product(factor_sub_one.T, mirrored_one), product(mirrored_one.T...]
    pallas_call x0 -> x4, Pallas kernels: none -> 154 us  [ancestor_product(): pl.pallas_call(ancestor_kernel, grid=(rows // tile,), out_shape=jax.Shape...]
    reduce_scatter x2 -> x0, waiting for transfers between devices: 90.6 us -> none  [row_sum(): lax.psum_scatter(partial_value, 'col', scatter_dimension=1, tiled=True)]
    ppermute x0 -> x20, waiting for transfers between devices: none -> 54.1 us  [exchange(): value = kept + lax.ppermute(outgoing, 'col', pairs)]
    another operation x0 -> x10, local copies, waits for them, and re-layouts: none -> 42.7 us  [the longest x5 31.7 us: per_device(): diag_part, link_part = device_sum(first)]
    dynamic_slice x8 -> x0, local copies, waits for them, and re-layouts: 34.4 us -> none  [the longest x4 25.9 us: mirror(): lax.dynamic_slice_in_dim(complete, parity * column_rows, column_rows, 0)]
    dot_general x0 -> x4, matrix products: none -> 33.2 us  [product_nt(): lax.dot_general(left, right, NT, precision=lax.Precision.HIGHEST, preferr...]
  transfers between devices with their start and end apart: 11 -> 34, of which waited for: 8 -> 18; matrix products, arithmetic and copies ran while one was open for 46% -> 19% of each run, Pallas kernels for 0% -> 19%
where the time goes in v1:
time: 820 us; the launch traced here: 814 us
  waiting for transfers between devices  333 us (41%)
  Pallas kernels  154 us (19%)
  local copies, waits for them, and re-layouts  102 us (12%)
  other arithmetic  68.8 us (8%)
  starting transfers between devices  55.7 us (7%)
  matrix products  54.8 us (7%)
  blocking collectives  30.6 us (4%)
  between operations  15.4 us (2%)
    all_gather x4, waiting for transfers between devices, factor(): lax.all_gather(part[:, q], 'row', axis=0, tiled=True)  174 us
    pallas_call x4, Pallas kernels, ancestor_product(): pl.pallas_call(ancestor_kernel, grid=(rows // tile,), out_shape=jax.Shape...  154 us
    ppermute x20, waiting for transfers between devices, exchange(): value = kept + lax.ppermute(outgoing, 'col', pairs)  54.1 us
    all_to_all x4, waiting for transfers between devices, mirror(): lax.all_to_all(outgoing, 'row', split_axis=0, concat_axis=0, tiled=True)  37.2 us
    dot_general x4, matrix products, product_nt(): lax.dot_general(left, right, NT, precision=lax.Precision.HIGHEST, preferr...  33.2 us
    all_to_all x3, waiting for transfers between devices, mirror(): lax.all_to_all(spread, 'col', split_axis=0, concat_axis=0, tiled=True)  32.3 us
    another operation x5, local copies, waits for them, and re-layouts, per_device(): diag_part, link_part = device_sum(first)  31.7 us
    select_n x2, other arithmetic, factor(): jnp.repeat(-mask_part.astype(jnp.float32), BLOCK, total_repeat_length=col...  30.3 us
  transfers between devices with their start and end apart: 34, of which 18 were waited for; matrix products, arithmetic and copies ran while one was open for 19% of the time, Pallas kernels for 19%

profile of v1, /device:TPU:0, one launch (start us, length us, event | category | flops | bytes accessed | tf_op | source)
XLA Modules:
  0.0 813.7 jit_solution(3890858857481244070)
XLA Ops:
  11.2 15.2 %select_select_fusion = f32[3072]{0:T(1024)S(1)} fusion(f32[]{:T(128)} %bitcast.82, f32[]{:T(128)} %bitcast.81, f32[]{:T(128)} %bitcast.80, f32[]{:T(128)} %bitcast.79, f32[]{:T(128)} %bitcast.78, f32[]{:T(128)} %bitcast.77, f32[]{:T(128)} %bitcast.76, f32[]{:T(128)} %bitcast.75, f32[]{:T(128)} %bitcast.74, f32[]{:T(128)} %bitcast.73, f32[]{:T(128)} %bitcast.72, ...), kind=kLoop, calls=%fused_computation.73 | loop fusion | flops 168960 | bytes 12384 | tf_op jit(solution)/shard_map/jit(_take)/select_n | solution.py:85
  30.0 15.1 %select_select_fusion.1 = f32[3072]{0:T(1024)S(1)} fusion(f32[]{:T(128)} %bitcast.24, f32[]{:T(128)} %bitcast.23, f32[]{:T(128)} %bitcast.22, f32[]{:T(128)} %bitcast.21, f32[]{:T(128)} %bitcast.20, f32[]{:T(128)} %bitcast.19, f32[]{:T(128)} %bitcast.18, f32[]{:T(128)} %bitcast.17, f32[]{:T(128)} %bitcast.16, f32[]{:T(128)} %bitcast.15, f32[]{:T(128)} %bitcast.14, ...), kind=kLoop, calls=%fused_computation.74 | loop fusion | flops 168960 | bytes 12384 | tf_op jit(solution)/shard_map/jit(_take)/select_n | solution.py:85
  49.3 44.9 %all-gather.19.cloned.1.call-done = f32[8,1,32,3072]{3,2,1,0:T(8,128)} async-done(((f32[2,1,32,3072]{3,2,1,0:T(8,128)}), f32[8,1,32,3072]{3,2,1,0:T(8,128)}) %all-gather.19.cloned.1.call-update) | async-done | bytes 3145744 | tf_op jit(solution)/shard_map/all_gather | solution.py:89
  94.2 64.4 %all-gather.15.cloned.1.call-done = f32[8,1,32,3072]{3,2,1,0:T(8,128)} async-done(((f32[2,1,32,3072]{3,2,1,0:T(8,128)}), f32[8,1,32,3072]{3,2,1,0:T(8,128)}) %all-gather.15.cloned.1.call-update) | async-done | bytes 3145744 | tf_op jit(solution)/shard_map/all_gather | solution.py:89
  158.6 64.3 %all-gather.17.cloned.1.call-done = f32[8,1,32,3072]{3,2,1,0:T(8,128)} async-done(((f32[2,1,32,3072]{3,2,1,0:T(8,128)}), f32[8,1,32,3072]{3,2,1,0:T(8,128)}) %all-gather.17.cloned.1.call-update) | async-done | bytes 3145744 | tf_op jit(solution)/shard_map/all_gather | solution.py:89
  222.9 8.4 %fusion.factor_ref = f32[256,3072]{1,0:T(8,128)S(1)} fusion(f32[256,3072]{1,0:T(8,128)} %bitcast.363, f32[256,512]{1,0:T(8,128)S(1)} %bitcast.399, f32[256,3072]{1,0:T(8,128)} %bitcast.359, f32[256,3072]{1,0:T(8,128)} %bitcast.355), kind=kOutput, calls=%fused_computation.4 | convolution fusion | flops 4834197504 | bytes 13107200 | tf_op jit(solution)/shard_map/dot_general | solution.py:16
  231.3 38.8 %shard_map.121 = f32[256,6144]{1,0:T(8,128)} custom-call(f32[256,3072]{1,0:T(8,128)S(1)} %fusion.factor_ref, f32[6144,3072]{1,0:T(8,128)} %ancestor_ref.7), custom_call_target="tpu_custom_call" | custom-call | flops 28991029248 | bytes 84934656 | tf_op jit(solution)/shard_map/pallas_call | solution.py:51
  274.1 38.3 %shard_map.119 = f32[256,6144]{1,0:T(8,128)} custom-call(f32[256,3072]{1,0:T(8,128)S(1)} %bitcast.356, f32[6144,3072]{1,0:T(8,128)} %ancestor_ref.7), custom_call_target="tpu_custom_call" | custom-call | flops 28991029248 | bytes 84934656 | tf_op jit(solution)/shard_map/pallas_call | solution.py:51
  312.4 8.0 fusion.1.factor_ref
  320.4 38.6 %shard_map.122 = f32[256,6144]{1,0:T(8,128)} custom-call(f32[256,3072]{1,0:T(8,128)S(1)} %fusion.1.factor_ref, f32[6144,3072]{1,0:T(8,128)} %ancestor_ref.7), custom_call_target="tpu_custom_call" | custom-call | flops 28991029248 | bytes 84934656 | tf_op jit(solution)/shard_map/pallas_call | solution.py:51
  366.4 38.3 %shard_map.120 = f32[256,6144]{1,0:T(8,128)} custom-call(f32[256,3072]{1,0:T(8,128)S(1)} %bitcast.362, f32[6144,3072]{1,0:T(8,128)} %ancestor_ref.7), custom_call_target="tpu_custom_call" | custom-call | flops 28991029248 | bytes 84934656 | tf_op jit(solution)/shard_map/pallas_call | solution.py:51
  433.8 15.3 %collective-permute-done.16 = f32[2,16,6144]{2,1,0:T(8,128)} collective-permute-done((f32[2,16,6144]{2,1,0:T(8,128)}, f32[2,16,6144]{2,1,0:T(8,128)}, u32[]{:S(2)}, u32[]{:S(2)}) %collective-permute-start.16) | collective-permute-done | bytes 786464 | tf_op jit(solution)/shard_map/ppermute | solution.py:101
  454.4 11.5 %collective-permute-done.1 = f32[2,16,6144]{2,1,0:T(8,128)S(1)} collective-permute-done((f32[2,16,6144]{2,1,0:T(8,128)S(1)}, f32[2,16,6144]{2,1,0:T(8,128)S(1)}, u32[]{:S(2)}, u32[]{:S(2)}) %collective-permute-start.1) | collective-permute-done | bytes 786464 | tf_op jit(solution)/shard_map/ppermute | solution.py:101
  471.7 11.1 %collective-permute-done.6 = f32[2,16,6144]{2,1,0:T(8,128)S(1)} collective-permute-done((f32[2,16,6144]{2,1,0:T(8,128)S(1)}, f32[2,16,6144]{2,1,0:T(8,128)S(1)}, u32[]{:S(2)}, u32[]{:S(2)}) %collective-permute-start.6) | collective-permute-done | bytes 786464 | tf_op jit(solution)/shard_map/ppermute | solution.py:101
  529.2 15.6 %all-to-all-done.7 = f32[4,8,6144]{2,1,0:T(8,128)} async-done(((f32[4,8,6144]{2,1,0:T(8,128)}), f32[4,8,6144]{2,1,0:T(8,128)}, u32[]{:S(2)}, u32[]{:S(2)}) %all-to-all-start.7) | async-done | bytes 786464 | tf_op jit(solution)/shard_map/all_to_all | solution.py:115
  551.2 10.5 %all-to-all-done.6 = f32[8,8,3072]{2,1,0:T(8,128)} async-done(((f32[8,8,3072]{2,1,0:T(8,128)}), f32[8,8,3072]{2,1,0:T(8,128)}, u32[]{:S(2)}, u32[]{:S(2)}) %all-to-all-start.6) | async-done | bytes 786464 | tf_op jit(solution)/shard_map/all_to_all | solution.py:118
  567.9 10.6 %all-to-all-done.8 = f32[8,8,3072]{2,1,0:T(8,128)} async-done(((f32[8,8,3072]{2,1,0:T(8,128)}), f32[8,8,3072]{2,1,0:T(8,128)}, u32[]{:S(2)}, u32[]{:S(2)}) %all-to-all-start.8) | async-done | bytes 786464 | tf_op jit(solution)/shard_map/all_to_all | solution.py:118
  584.6 9.3 %fusion.3 = f32[64,512]{1,0:T(8,128)S(1)} fusion(f32[256,3072]{1,0:T(8,128)} %bitcast.368, f32[256,3072]{1,0:T(8,128)} %bitcast.364, f32[8,8,3072]{2,1,0:T(8,128)} %all-to-all-done.6), kind=kOutput, calls=%fused_computation.7 | convolution fusion | flops 1209532416 | bytes 7208960 | tf_op jit(solution)/shard_map/dot_general | solution.py:20
  593.9 7.3 fusion.2
  621.6 16.3 %all-to-all-done.2 = f32[4,8,6144]{2,1,0:T(8,128)} async-done(((f32[4,8,6144]{2,1,0:T(8,128)}), f32[4,8,6144]{2,1,0:T(8,128)}, u32[]{:S(2)}, u32[]{:S(2)}) %all-to-all-start.2) | async-done | bytes 786464 | tf_op jit(solution)/shard_map/all_to_all | solution.py:115
  644.3 11.3 %all-to-all-done.1 = f32[8,8,3072]{2,1,0:T(8,128)} async-done(((f32[8,8,3072]{2,1,0:T(8,128)}), f32[8,8,3072]{2,1,0:T(8,128)}, u32[]{:S(2)}, u32[]{:S(2)}) %all-to-all-start.1) | async-done | bytes 786464 | tf_op jit(solution)/shard_map/all_to_all | solution.py:118
  655.5 18.1 %all_to_all.50 = f32[8,8,3072]{2,1,0:T(8,128)S(1)} all-to-all(f32[8,8,3072]{2,1,0:T(8,128)} %bitcast.397), channel_id=1, replica_groups=mesh['row'=4,'col'=8] {'col'}, dimensions={0} | all-to-all | bytes 1572864 | tf_op jit(solution)/shard_map/all_to_all | solution.py:118
  673.7 8.9 %fusion.5 = f32[128,512]{1,0:T(8,128)S(1)} fusion(f32[256,3072]{1,0:T(8,128)} %bitcast.361, f32[256,3072]{1,0:T(8,128)S(1)} %bitcast.358, f32[64,3072]{1,0:T(8,128)S(1)} %bitcast.374, f32[64,3072]{1,0:T(8,128)} %bitcast.55), kind=kOutput, calls=%fused_computation.9 | convolution fusion | flops 2417885184 | bytes 8126464 | tf_op jit(solution)/shard_map/dot_general | solution.py:20
  682.6 7.8 fusion.4
  690.5 12.5 %all_to_all.51 = f32[8,16,1024]{2,1,0:T(8,128)S(1)} all-to-all(f32[8,16,1024]{2,1,0:T(8,128)S(1)} %bitcast.400), channel_id=1, replica_groups=mesh['row'=4,'col'=8] {'col'}, dimensions={0} | all-to-all | bytes 1048576 | tf_op jit(solution)/shard_map/all_to_all | solution.py:124
  715.2 6.8 copy.57
  728.2 29.2 %all-gather.11.cloned.1.call-done = f32[512,1024]{1,0:T(8,128)} async-done(((f32[16,1024]{1,0:T(8,128)}), f32[512,1024]{1,0:T(8,128)}) %all-gather.11.cloned.1.call-update) | async-done | bytes 2097168 | tf_op jit(solution)/shard_map/all_gather | solution.py:126
  757.4 6.5 reshape.178
  763.9 6.4 fusion.42
  774.5 7.2 unstack.13
  781.7 6.8 copy.55
  788.5 7.2 unstack.15
  (219 shorter events, 188.0 us)
Async XLA Ops:
  7.2 87.0 %all-gather.19.cloned.1.call-start = ((), (), s32[]{:S(2)}) async-start(), calls=%async_computation.14 | async-start | bytes 3932160 | tf_op jit(solution)/shard_map/all_gather | solution.py:89
  27.8 130.7 %all-gather.15.cloned.1.call-start = ((), (), s32[]{:S(2)}) async-start(), calls=%async_computation.12 | async-start | bytes 3932160 | tf_op jit(solution)/shard_map/all_gather | solution.py:89
  46.6 176.3 %all-gather.17.cloned.1.call-start = ((), (), s32[]{:S(2)}) async-start(), calls=%async_computation.13 | async-start | bytes 3932160 | tf_op jit(solution)/shard_map/all_gather | solution.py:89
  47.4 265.0 %all-gather.21.cloned.1.call-start = ((), (), s32[]{:S(2)}) async-start(), calls=%async_computation.15 | async-start | bytes 3932160 | tf_op jit(solution)/shard_map/all_gather | solution.py:89
  274.1 132.9 %collective-permute-start.10 = (f32[2,2,32,6144]{3,2,1,0:T(8,128)}, f32[2,2,32,6144]{3,2,1,0:T(8,128)}, u32[]{:S(2)}, u32[]{:S(2)}) collective-permute-start(f32[2,2,32,6144]{3,2,1,0:T(8,128)} %dynamic-slice_bitcast_fusion.1), channel_id=1, source_target_pairs={{0,1},{1,0},{2,3},{3,2},{4,5},{5,4},{6,7},{7,6},{8,9},{9,8},{10,11... | collective-permute-start | bytes 9437192 | tf_op jit(solution)/shard_map/ppermute | solution.py:101
  362.9 52.7 %collective-permute-start.15 = (f32[2,2,32,6144]{3,2,1,0:T(8,128)}, f32[2,2,32,6144]{3,2,1,0:T(8,128)}, u32[]{:S(2)}, u32[]{:S(2)}) collective-permute-start(f32[2,2,32,6144]{3,2,1,0:T(8,128)} %dynamic-slice_bitcast_fusion), channel_id=1, source_target_pairs={{0,1},{1,0},{2,3},{3,2},{4,5},{5,4},{6,7},{7,6},{8,9},{9,8},{10,11... | collective-permute-start | bytes 9437192 | tf_op jit(solution)/shard_map/ppermute | solution.py:101
  365.3 55.3 %collective-permute-start = (f32[2,2,32,6144]{3,2,1,0:T(8,128)}, f32[2,2,32,6144]{3,2,1,0:T(8,128)}, u32[]{:S(2)}, u32[]{:S(2)}) collective-permute-start(f32[2,2,32,6144]{3,2,1,0:T(8,128)} %dynamic-slice_bitcast_fusion.3), channel_id=1, source_target_pairs={{0,1},{1,0},{2,3},{3,2},{4,5},{5,4},{6,7},{7,6},{8,9},{9,8},{10,11... | collective-permute-start | bytes 9437192 | tf_op jit(solution)/shard_map/ppermute | solution.py:101
  406.9 17.0 %collective-permute-start.5 = (f32[2,2,32,6144]{3,2,1,0:T(8,128)S(1)}, f32[2,2,32,6144]{3,2,1,0:T(8,128)S(1)}, u32[]{:S(2)}, u32[]{:S(2)}) collective-permute-start(f32[2,2,32,6144]{3,2,1,0:T(8,128)S(1)} %dynamic-slice_bitcast_fusion.2), channel_id=1, source_target_pairs={{0,1},{1,0},{2,3},{3,2},{4,5},{5,4},{6,7},{7,6},{8,9},{9,8},{10,11... | collective-permute-start | bytes 9437192 | tf_op jit(solution)/shard_map/ppermute | solution.py:101
  411.6 20.6 %collective-permute-start.11 = (f32[2,16,6144]{2,1,0:T(8,128)}, f32[2,16,6144]{2,1,0:T(8,128)S(1)}, u32[]{:S(2)}, u32[]{:S(2)}) collective-permute-start(f32[2,16,6144]{2,1,0:T(8,128)} %dynamic-slice_bitcast_fusion.7), channel_id=1, source_target_pairs={{0,2},{1,3},{2,0},{3,1},{4,6},{5,7},{6,4},{7,5},{8,10},{9,11},{10,... | collective-permute-start | bytes 2359304 | tf_op jit(solution)/shard_map/ppermute | solution.py:101
  414.1 37.8 %collective-permute-start.13 = (f32[2,16,6144]{2,1,0:T(8,128)}, f32[2,16,6144]{2,1,0:T(8,128)S(1)}, u32[]{:S(2)}, u32[]{:S(2)}) collective-permute-start(f32[2,16,6144]{2,1,0:T(8,128)} %dynamic-slice_bitcast_fusion.6), channel_id=1, source_target_pairs={{0,4},{1,5},{2,6},{3,7},{4,0},{5,1},{6,2},{7,3},{8,12},{9,13},{10,... | collective-permute-start | bytes 2359304 | tf_op jit(solution)/shard_map/ppermute | solution.py:101
  419.1 30.0 %collective-permute-start.16 = (f32[2,16,6144]{2,1,0:T(8,128)}, f32[2,16,6144]{2,1,0:T(8,128)}, u32[]{:S(2)}, u32[]{:S(2)}) collective-permute-start(f32[2,16,6144]{2,1,0:T(8,128)} %dynamic-slice_bitcast_fusion.5), channel_id=1, source_target_pairs={{0,2},{1,3},{2,0},{3,1},{4,6},{5,7},{6,4},{7,5},{8,10},{9,11},{10,... | collective-permute-start | bytes 2359304 | tf_op jit(solution)/shard_map/ppermute | solution.py:101
  420.6 33.0 %collective-permute-start.18 = (f32[2,16,6144]{2,1,0:T(8,128)}, f32[2,16,6144]{2,1,0:T(8,128)S(1)}, u32[]{:S(2)}, u32[]{:S(2)}) collective-permute-start(f32[2,16,6144]{2,1,0:T(8,128)} %dynamic-slice_bitcast_fusion.4), channel_id=1, source_target_pairs={{0,4},{1,5},{2,6},{3,7},{4,0},{5,1},{6,2},{7,3},{8,12},{9,13},{10,... | collective-permute-start | bytes 2359304 | tf_op jit(solution)/shard_map/ppermute | solution.py:101
  423.9 41.9 %collective-permute-start.1 = (f32[2,16,6144]{2,1,0:T(8,128)S(1)}, f32[2,16,6144]{2,1,0:T(8,128)S(1)}, u32[]{:S(2)}, u32[]{:S(2)}) collective-permute-start(f32[2,16,6144]{2,1,0:T(8,128)S(1)} %dynamic-slice_bitcast_fusion.11), channel_id=1, source_target_pairs={{0,2},{1,3},{2,0},{3,1},{4,6},{5,7},{6,4},{7,5},{8,10},{9,11},{10,... | collective-permute-start | bytes 2359304 | tf_op jit(solution)/shard_map/ppermute | solution.py:101
  432.2 36.2 %collective-permute-start.3 = (f32[2,16,6144]{2,1,0:T(8,128)S(1)}, f32[2,16,6144]{2,1,0:T(8,128)S(1)}, u32[]{:S(2)}, u32[]{:S(2)}) collective-permute-start(f32[2,16,6144]{2,1,0:T(8,128)S(1)} %dynamic-slice_bitcast_fusion.10), channel_id=1, source_target_pairs={{0,4},{1,5},{2,6},{3,7},{4,0},{5,1},{6,2},{7,3},{8,12},{9,13},{10,... | collective-permute-start | bytes 2359304 | tf_op jit(solution)/shard_map/ppermute | solution.py:101
  449.1 33.6 %collective-permute-start.6 = (f32[2,16,6144]{2,1,0:T(8,128)S(1)}, f32[2,16,6144]{2,1,0:T(8,128)S(1)}, u32[]{:S(2)}, u32[]{:S(2)}) collective-permute-start(f32[2,16,6144]{2,1,0:T(8,128)S(1)} %dynamic-slice_bitcast_fusion.9), channel_id=1, source_target_pairs={{0,2},{1,3},{2,0},{3,1},{4,6},{5,7},{6,4},{7,5},{8,10},{9,11},{10,... | collective-permute-start | bytes 2359304 | tf_op jit(solution)/shard_map/ppermute | solution.py:101
  451.9 34.2 %collective-permute-start.8 = (f32[2,16,6144]{2,1,0:T(8,128)S(1)}, f32[2,16,6144]{2,1,0:T(8,128)S(1)}, u32[]{:S(2)}, u32[]{:S(2)}) collective-permute-start(f32[2,16,6144]{2,1,0:T(8,128)S(1)} %dynamic-slice_bitcast_fusion.8), channel_id=1, source_target_pairs={{0,4},{1,5},{2,6},{3,7},{4,0},{5,1},{6,2},{7,3},{8,12},{9,13},{10,... | collective-permute-start | bytes 2359304 | tf_op jit(solution)/shard_map/ppermute | solution.py:101
  453.6 40.1 %collective-permute-start.12 = (f32[16,6144]{1,0:T(8,128)S(1)}, f32[16,6144]{1,0:T(8,128)S(1)}, u32[]{:S(2)}, u32[]{:S(2)}) collective-permute-start(f32[16,6144]{1,0:T(8,128)S(1)} %dynamic-slice_bitcast_fusion.15), channel_id=1, source_target_pairs={{0,4},{1,5},{2,6},{3,7},{4,0},{5,1},{6,2},{7,3},{8,12},{9,13},{10,... | collective-permute-start | bytes 1179656 | tf_op jit(solution)/shard_map/ppermute | solution.py:101
  465.9 28.3 %collective-permute-start.14 = (f32[16,6144]{1,0:T(8,128)S(1)}, f32[16,6144]{1,0:T(8,128)S(1)}, u32[]{:S(2)}, u32[]{:S(2)}) collective-permute-start(f32[16,6144]{1,0:T(8,128)S(1)} %dynamic-slice_bitcast_fusion.14), channel_id=1, source_target_pairs={{0,2},{1,3},{2,0},{3,1},{4,6},{5,7},{6,4},{7,5},{8,10},{9,11},{10,... | collective-permute-start | bytes 1179656 | tf_op jit(solution)/shard_map/ppermute | solution.py:101
  468.4 33.8 %collective-permute-start.17 = (f32[16,6144]{1,0:T(8,128)}, f32[16,6144]{1,0:T(8,128)}, u32[]{:S(2)}, u32[]{:S(2)}) collective-permute-start(f32[16,6144]{1,0:T(8,128)} %dynamic-slice_bitcast_fusion.13), channel_id=1, source_target_pairs={{0,4},{1,5},{2,6},{3,7},{4,0},{5,1},{6,2},{7,3},{8,12},{9,13},{10,... | collective-permute-start | bytes 1179656 | tf_op jit(solution)/shard_map/ppermute | solution.py:101
  482.7 21.8 %collective-permute-start.19 = (f32[16,6144]{1,0:T(8,128)}, f32[16,6144]{1,0:T(8,128)}, u32[]{:S(2)}, u32[]{:S(2)}) collective-permute-start(f32[16,6144]{1,0:T(8,128)} %dynamic-slice_bitcast_fusion.12), channel_id=1, source_target_pairs={{0,2},{1,3},{2,0},{3,1},{4,6},{5,7},{6,4},{7,5},{8,10},{9,11},{10,... | collective-permute-start | bytes 1179656 | tf_op jit(solution)/shard_map/ppermute | solution.py:101
  486.0 24.6 %collective-permute-start.2 = (f32[16,6144]{1,0:T(8,128)}, f32[16,6144]{1,0:T(8,128)}, u32[]{:S(2)}, u32[]{:S(2)}) collective-permute-start(f32[16,6144]{1,0:T(8,128)} %dynamic-slice_bitcast_fusion.19), channel_id=1, source_target_pairs={{0,4},{1,5},{2,6},{3,7},{4,0},{5,1},{6,2},{7,3},{8,12},{9,13},{10,... | collective-permute-start | bytes 1179656 | tf_op jit(solution)/shard_map/ppermute | solution.py:101
  493.6 18.9 %collective-permute-start.4 = (f32[16,6144]{1,0:T(8,128)}, f32[16,6144]{1,0:T(8,128)}, u32[]{:S(2)}, u32[]{:S(2)}) collective-permute-start(f32[16,6144]{1,0:T(8,128)} %dynamic-slice_bitcast_fusion.18), channel_id=1, source_target_pairs={{0,2},{1,3},{2,0},{3,1},{4,6},{5,7},{6,4},{7,5},{8,10},{9,11},{10,... | collective-permute-start | bytes 1179656 | tf_op jit(solution)/shard_map/ppermute | solution.py:101
  494.2 31.0 %collective-permute-start.7 = (f32[16,6144]{1,0:T(8,128)}, f32[16,6144]{1,0:T(8,128)}, u32[]{:S(2)}, u32[]{:S(2)}) collective-permute-start(f32[16,6144]{1,0:T(8,128)} %dynamic-slice_bitcast_fusion.17), channel_id=1, source_target_pairs={{0,4},{1,5},{2,6},{3,7},{4,0},{5,1},{6,2},{7,3},{8,12},{9,13},{10,... | collective-permute-start | bytes 1179656 | tf_op jit(solution)/shard_map/ppermute | solution.py:101
  497.6 23.0 %all-to-all-start.5 = ((f32[4,8,6144]{2,1,0:T(8,128)}), f32[4,8,6144]{2,1,0:T(8,128)}, u32[]{:S(2)}, u32[]{:S(2)}) async-start(f32[4,8,6144]{2,1,0:T(8,128)} %maximum_bitcast_fusion.4), calls=%async_computation.5 | async-start | bytes 1572864 | tf_op jit(solution)/shard_map/all_to_all | solution.py:115
  502.2 80.5 %collective-permute-start.9 = (f32[16,6144]{1,0:T(8,128)}, f32[16,6144]{1,0:T(8,128)}, u32[]{:S(2)}, u32[]{:S(2)}) collective-permute-start(f32[16,6144]{1,0:T(8,128)} %dynamic-slice_bitcast_fusion.16), channel_id=1, source_target_pairs={{0,2},{1,3},{2,0},{3,1},{4,6},{5,7},{6,4},{7,5},{8,10},{9,11},{10,... | collective-permute-start | bytes 1179656 | tf_op jit(solution)/shard_map/ppermute | solution.py:101
  520.5 24.3 %all-to-all-start.7 = ((f32[4,8,6144]{2,1,0:T(8,128)}), f32[4,8,6144]{2,1,0:T(8,128)}, u32[]{:S(2)}, u32[]{:S(2)}) async-start(f32[4,8,6144]{2,1,0:T(8,128)} %maximum_bitcast_fusion.5), calls=%async_computation.7 | async-start | bytes 1572864 | tf_op jit(solution)/shard_map/all_to_all | solution.py:115
  544.8 16.8 %all-to-all-start.6 = ((f32[8,8,3072]{2,1,0:T(8,128)}), f32[8,8,3072]{2,1,0:T(8,128)}, u32[]{:S(2)}, u32[]{:S(2)}) async-start(f32[8,8,3072]{2,1,0:T(8,128)} %bitcast.395), calls=%async_computation.6 | async-start | bytes 1572864 | tf_op jit(solution)/shard_map/all_to_all | solution.py:118
  578.5 23.4 %all-to-all-start = ((f32[4,8,6144]{2,1,0:T(8,128)}), f32[4,8,6144]{2,1,0:T(8,128)}, u32[]{:S(2)}, u32[]{:S(2)}) async-start(f32[4,8,6144]{2,1,0:T(8,128)} %maximum_bitcast_fusion.2), calls=%async_computation | async-start | bytes 1572864 | tf_op jit(solution)/shard_map/all_to_all | solution.py:115
  612.9 25.0 %all-to-all-start.2 = ((f32[4,8,6144]{2,1,0:T(8,128)}), f32[4,8,6144]{2,1,0:T(8,128)}, u32[]{:S(2)}, u32[]{:S(2)}) async-start(f32[4,8,6144]{2,1,0:T(8,128)} %maximum_bitcast_fusion.3), calls=%async_computation.2 | async-start | bytes 1572864 | tf_op jit(solution)/shard_map/all_to_all | solution.py:115
  617.9 93.5 %all-gather.13.cloned.1.call-start = ((), (), s32[]{:S(2)}) async-start(), calls=%async_computation.11 | async-start | bytes 1081344 | tf_op jit(solution)/shard_map/all_gather | solution.py:126
  637.9 17.7 %all-to-all-start.1 = ((f32[8,8,3072]{2,1,0:T(8,128)}), f32[8,8,3072]{2,1,0:T(8,128)}, u32[]{:S(2)}, u32[]{:S(2)}) async-start(f32[8,8,3072]{2,1,0:T(8,128)} %bitcast.394), calls=%async_computation.1 | async-start | bytes 1572864 | tf_op jit(solution)/shard_map/all_to_all | solution.py:118
  642.1 115.3 %all-gather.11.cloned.1.call-start = ((), (), s32[]{:S(2)}) async-start(), calls=%async_computation.10 | async-start | bytes 2162688 | tf_op jit(solution)/shard_map/all_gather | solution.py:126
  (36 other events, 383.3 us)
Sparse Core Ops, SparseCore 0:
  28.0 66.1 all-gather.18
  96.3 62.1 all-gather.14
  160.7 62.1 all-gather.16
  224.9 62.1 all-gather.20
  621.7 56.6 all-gather.12
  703.8 53.5 all-gather.10
